TPU v7x, 512 devices: a whole 4x8x8 slice. The times are simulated.
512 devices in a mesh: dp: 64 (over z_lo, y, core), mp: 8 (over z_hi, x).
Axes of the slice: x: 4, y: 8, z: 8 (z_hi: 2, z_lo: 4; z = z_hi * 4 + z_lo), core: 2. Of those that a mesh axis runs over, the one named last changes fastest.
Arguments:
- inputs: bfloat16 [30720, 192], P('dp'), may hold values from -80 to 80
- cotangent: bfloat16 [30720, 36864], P('dp', 'mp'), may hold values from -80 to 80
- matrix: float32 [192, 36864], P('dp', 'mp'), may hold values from -60 to 60
- momentum: float32 [192, 36864], P('dp', 'mp'), may hold values from -0.4375 to 0.4375
- row_factor: float32 [192], P('dp'), as said below
- col_factor: float32 [36864], P('mp'), may hold values from 0.010368 to 30.72
- row_rest: float32 [192], P('dp'), may hold values from 36864 to 14745600
- col_rest: float32 [36864], P('mp'), may hold values from 192 to 576000
Outputs:
- new_matrix: float32 [192, 36864], P('dp', 'mp')
- new_momentum: float32 [192, 36864], P('dp', 'mp')
- new_row: float32 [192], P('dp')
- new_col: float32 [36864], P('mp')
Inputs may be any that keep to these rules, and one draw needn't show every extreme that they name: `row_factor`: each entry is positive.
All inputs are finite; a program needn't handle non-finite values.
Results may differ from a plain program's by a relative error of at most 0.0003.
Values sent between devices are 32-bit elements; how exact they have to be, the bound alone decides.
A program may use at most 64 MiB of HBM per device.

v0:
```python
import jax
import jax.numpy as jnp
from jax import lax
from jax.sharding import PartitionSpec as P

FULL_ROWS = 18432
FULL_COLS = 73728


beta_two = 1.0 - 10.0 ** (-0.8)
beta_one = 0.9
rel_step = 0.01
eps_sq = 1e-30


def on_device(inputs, cotangent, matrix, momentum, row_factor, col_factor, row_rest, col_rest):
    local_rows = matrix.shape[0]
    total_rows = local_rows * lax.axis_size("dp")
    entries = float(total_rows) * float(matrix.shape[1] * lax.axis_size("mp"))
    contract = (((0,), (0,)), ((), ()))
    matrix_sq = lax.psum(jnp.sum(matrix * matrix), ("dp", "mp"))
    gradient = lax.psum_scatter(
        lax.dot_general(inputs, cotangent, contract, preferred_element_type=jnp.float32),
        "dp",
        scatter_dimension=0,
        tiled=True,
    )
    squares = gradient * gradient + eps_sq
    column_sum = lax.psum(jnp.sum(squares, axis=0), "dp")
    row_sum = lax.psum(jnp.sum(squares, axis=1), "mp")
    new_row = beta_two * row_factor + (1.0 - beta_two) * ((row_sum + row_rest) / FULL_COLS)
    new_col = beta_two * col_factor + (1.0 - beta_two) * ((column_sum + col_rest) / FULL_ROWS)
    inverse_col = lax.rsqrt(new_col)
    row_total = lax.psum(jnp.sum(new_row), "dp")
    row_mean = row_total / total_rows
    scaled = gradient * lax.rsqrt(new_row / row_mean)[:, None] * inverse_col[None, :]
    matrix_rms = jnp.sqrt(matrix_sq / entries)
    new_momentum = beta_one * momentum + (1.0 - beta_one) * rel_step * matrix_rms * scaled
    new_matrix = matrix - new_momentum
    return (new_matrix, new_momentum, new_row, new_col)


def solution(mesh):
    placed = (
        P("dp", None),
        P("dp", "mp"),
        P("dp", "mp"),
        P("dp", "mp"),
        P("dp"),
        P("mp"),
        P("dp"),
        P("mp"),
    )
    return jax.shard_map(
        on_device,
        mesh=mesh,
        in_specs=placed,
        out_specs=(P("dp", "mp"), P("dp", "mp"), P("dp"), P("mp")),
        check_vma=False,
    )
```

profile of v0, /device:TPU:1, one launch (start us, length us, event | category | flops | bytes accessed | tf_op | source)
XLA Modules:
  0.0 868.2 jit_solution(12347820840780088302)
XLA Ops:
  7.2 0.0 copy-start
  7.2 0.0 all-reduce.4.cloned.1.call-start
  7.2 0.9 copy-done
  8.1 5.1 fusion.5
  13.2 0.0 copy-start.1
  13.2 0.0 copy-start.5
  13.2 0.0 copy-start.6
  13.2 0.0 copy-start.3
  13.3 0.0 copy-start.4
  13.3 0.0 copy-start.2
  13.3 0.0 all-reduce.4.cloned.1.call-update
  13.3 0.8 copy-done.1
  14.1 0.6 multiply_reduce_fusion
  14.8 107.7 %psum.28 = f32[]{:T(128)} all-reduce(f32[]{:T(128)} %multiply_reduce_fusion), channel_id=1, replica_groups=mesh['dp'=64,'mp'=8] {'dp','mp'}, use_global_device_ids=true, to_apply=%region_1.0 | all-reduce | flops 1 | bytes 8 | tf_op jit(solution)/shard_map/psum | solution.py:21
  123.1 1.3 dynamic-slice
  125.1 435.6 %all-reduce.4.cloned.1.call-done = f32[192,4608]{1,0:T(8,128)} async-done(((f32[192,4608]{1,0:T(8,128)}), f32[192,4608]{1,0:T(8,128)}) %all-reduce.4.cloned.1.call-update) | async-done | bytes 3538960
  560.7 1.1 fusion.1
  561.8 27.3 %psum.29 = f32[3]{0:T(128)S(1)} all-reduce(f32[3]{0:T(128)S(1)} %get-tuple-element.4), channel_id=1, replica_groups=mesh['dp'=64,'mp'=8] {'mp'}, use_global_device_ids=true, to_apply=%region_4.0 | all-reduce | flops 3 | bytes 24 | tf_op jit(solution)/shard_map/psum | solution.py:30
  589.2 0.0 copy-done.5
  589.2 0.0 copy-done.6
  589.2 0.6 fusion.4
  589.8 0.0 copy-start.7
  589.8 268.6 %all-reduce.1 = (f32[4608]{0:T(1024)S(1)}, f32[]{:T(128)}) all-reduce(f32[4608]{0:T(1024)S(1)} %get-tuple-element.5, f32[]{:T(128)} %get-tuple-element.12), channel_id=1, replica_groups=mesh['dp'=64,'mp'=8] {'dp'}, use_global_device_ids=true, to_apply=%region_8.0 | all-reduce | flops 4609 | bytes 36872 | tf_op jit(solution)/shard_map/psum | solution.py:29
  859.0 0.0 copy-done.3
  859.0 0.0 copy-done.4
  859.0 0.6 fusion.3
  859.6 0.0 copy-done.2
  859.6 1.7 fusion.2
  861.4 0.0 copy-done.7
  (1 shorter events, 0.0 us)
Async XLA Ops:
  7.2 0.9 copy-start
  7.2 553.5 %all-reduce.4.cloned.1.call-start = ((), (), s32[]{:S(2)}) async-start(), calls=%async_computation | async-start | bytes 7077888
  13.2 0.9 copy-start.1
  13.2 575.9 %copy-start.5 = (f32[3]{0:T(128)S(1)}, f32[3]{0:T(128)}, u32[]{:S(2)}) copy-start(f32[3]{0:T(128)} %param.14) | copy-start | bytes 40
  13.2 575.9 %copy-start.6 = (f32[3]{0:T(128)S(1)}, f32[3]{0:T(128)}, u32[]{:S(2)}) copy-start(f32[3]{0:T(128)} %param.12) | copy-start | bytes 40
  13.2 845.8 %copy-start.3 = (f32[4608]{0:T(1024)S(1)}, f32[4608]{0:T(1024)}, u32[]{:S(2)}) copy-start(f32[4608]{0:T(1024)} %param.15) | copy-start | bytes 55300
  13.3 845.8 %copy-start.4 = (f32[4608]{0:T(1024)S(1)}, f32[4608]{0:T(1024)}, u32[]{:S(2)}) copy-start(f32[4608]{0:T(1024)} %param.13) | copy-start | bytes 55300
  13.3 846.4 %copy-start.2 = (f32[3,4608]{1,0:T(4,128)S(1)}, f32[3,4608]{1,0:T(4,128)}, u32[]{:S(2)}) copy-start(f32[3,4608]{1,0:T(4,128)} %param.11) | copy-start | bytes 165892
  589.8 271.6 %copy-start.7 = (f32[3]{0:T(128)}, f32[3]{0:T(128)S(1)}, u32[]{:S(2)}) copy-start(f32[3]{0:T(128)S(1)} %get-tuple-element.13) | copy-start | bytes 40
Sparse Core Ops, SparseCore 0:
  13.4 547.2 all-reduce.3
where the time goes:
time: 869 us; the launch traced here: 868 us
  waiting for transfers between devices  436 us (50%)
  blocking collectives  404 us (46%)
  between operations  16.1 us (2%)
    unnamed x2, waiting for transfers between devices  436 us
    psum x1, blocking collectives, on_device(): column_sum = lax.psum(jnp.sum(squares, axis=0), 'dp')  269 us
    psum x1, blocking collectives, on_device(): matrix_sq = lax.psum(jnp.sum(matrix * matrix), ('dp', 'mp'))  108 us
    psum x1, blocking collectives, on_device(): row_sum = lax.psum(jnp.sum(squares, axis=1), 'mp')  27.3 us
  transfers between devices with their start and end apart: 1, of which 1 were waited for; matrix products, arithmetic and copies ran while one was open for 0% of the time, Pallas kernels for 0%

commit v1 on v0

v1 whole, which is shorter than its diff:
```python
import functools

import jax
import jax.numpy as jnp
from jax import lax
from jax.experimental import pallas as pl
from jax.experimental.pallas import tpu as pltpu
from jax.sharding import PartitionSpec as P

FULL_ROWS = 18432
FULL_COLS = 73728
ROWS = 192
BLOCK_COLS = 36864

beta_two = 1.0 - 10.0 ** (-0.8)
beta_one = 0.9
rel_step = 0.01
eps_sq = 1e-30

MESH = pl.DeviceIdType.MESH
F32 = jnp.float32
VMEM = pltpu.VMEM

LANE_TILES = 9
TILES = 27
CHUNK = TILES * 8
GROUP = LANE_TILES * 128
SPREAD = 32
STREAMS = ((0, 0, 1, 4), (1, 0, -1, 4), (0, 1, -1, 3), (1, 1, 1, 3))
GROUP_ORDER = (0, 1, 3, 2)
GATHERED = 4 * SPREAD
SUMS = GATHERED + 4 * 16


def send(src, dst, send_sem, recv_sem, target):
    return pltpu.make_async_remote_copy(
        src_ref=src, dst_ref=dst, send_sem=send_sem, recv_sem=recv_sem, device_id=target, device_id_type=MESH
    )


def reduce_kernel(
    inputs_hbm, cot_hbm, matrix_ref, row_factor_ref, row_rest_ref, out_ref,
    inp, lhs, cot, part, sib, ring, zrecv, spread, gathered, small, small_recv, m1, p1, m2, p2,
    in_sem, cot_sem, sib_ss, sib_rs, small_ss, small_rs, ring_ss, ring_rs, z_ss, z_rs, g_ss, g_rs,
    p1_ss, p1_rs, p2_ss, p2_rs,
):
    d = lax.axis_index("dp")
    m = lax.axis_index("mp")
    z = d // 16
    y = lax.rem(d // 2, 8)
    c = lax.rem(d, 2)
    h = y // 4
    q = lax.rem(y, 4)
    home = z // 2
    active = c == home

    def dev(zz, yy, cc, mm):
        return (zz * 16 + yy * 2 + cc, mm)

    def turn(v, k, n):
        return lax.rem(v + k + n, n)

    in_copy = pltpu.make_async_copy(inputs_hbm, inp, in_sem)
    in_copy.start()
    cot_copies = []
    for n, off in enumerate(GROUP_ORDER):
        g = turn(q, off, 4)
        copy = pltpu.make_async_copy(
            cot_hbm.at[:, pl.ds(pl.multiple_of(g * GROUP, 128), GROUP)], cot.at[n], cot_sem.at[n]
        )
        copy.start()
        cot_copies.append(copy)

    barrier = pltpu.get_barrier_semaphore()

    def hello(target):
        pl.semaphore_signal(barrier, inc=1, device_id=target, device_id_type=MESH)

    hello(dev(z, y, 1 - c, m))
    for dy in range(1, 8):
        for cc in range(2):
            hello(dev(z, turn(y, dy, 8), cc, m))

    @pl.when(active)
    def _():
        for dz in range(4):
            for dm in range(8):
                if dz or dm:
                    zz = turn(z, dz, 4)
                    hello(dev(zz, y, zz // 2, turn(m, dm, 8)))
        for i in range(2):
            hello(dev((1 - home) * 2 + i, y, c, m))

    @pl.when(jnp.logical_not(active))
    def _():
        for i in range(2):
            hello(dev(2 * c + i, y, c, m))

    row = lax.broadcasted_iota(jnp.int32, (ROWS, ROWS), 0)
    col = lax.broadcasted_iota(jnp.int32, (ROWS, ROWS), 1)
    block = (row * 2731) >> 16
    inner = row - block * 24
    want = block * 24 + 3 * (inner & 7) + (inner >> 3)
    pick = jnp.where(col == want, 1.0, 0.0).astype(jnp.bfloat16)
    in_copy.wait()
    lhs[...] = jnp.dot(pick, inp[...], preferred_element_type=F32).astype(jnp.bfloat16)

    mat = matrix_ref[...]
    msq = jnp.sum(jnp.sum(mat * mat, axis=0, keepdims=True), axis=1, keepdims=True)
    base = jnp.float32(0.0)
    for j in range(3):
        base = base + beta_two * row_factor_ref[j] + (1.0 - beta_two) * (row_rest_ref[j] * (1.0 / FULL_COLS))
    sub8 = lax.broadcasted_iota(jnp.int32, (8, 128), 0)
    lane8 = lax.broadcasted_iota(jnp.int32, (8, 128), 1)
    small[...] = jnp.where(sub8 == 2, msq, jnp.where(sub8 == 3, base, 0.0))

    def product(n):
        cot_copies[n].wait()
        g = turn(q, GROUP_ORDER[n], 4)
        acc = jnp.dot(lhs[...], cot[n], preferred_element_type=F32)
        for zh in range(2):
            for i in range(2):
                for hh in range(2):
                    r0 = ((zh * 2 + i) * 2 + hh) * 24
                    for j in range(3):
                        for lb in range(LANE_TILES):
                            t = j * LANE_TILES + lb
                            part[zh, hh * 4 + g, i, t * 8 : t * 8 + 8, :] = acc[
                                r0 + j * 8 : r0 + j * 8 + 8, lb * 128 : lb * 128 + 128
                            ]

    sibling = dev(z, y, 1 - c, m)

    def sib_copy(o):
        return send(part.at[1 - c, o], sib.at[o], sib_ss.at[o], sib_rs.at[o], sibling)

    small_copy = send(small, small_recv, small_ss, small_rs, sibling)

    def pass_on(n):
        for off in (4, 0):
            sib_copy(turn(y, GROUP_ORDER[n] + off, 8)).start()

    arrived = set()

    def arrive(k):
        k %= 8
        if k not in arrived:
            arrived.add(k)
            sib_copy(turn(y, k, 8)).wait_recv()

    def ring_copy(stream, s):
        i, kind, way, n = stream
        o = turn(y, (way * (n + 1 - s)) % 8, 8)
        return send(
            part.at[c, o, i],
            ring.at[i, kind, s - 1],
            ring_ss.at[i, kind, s - 1],
            ring_rs.at[i, kind, s - 1],
            dev(z, turn(y, way % 8, 8), c, m),
        )

    def ring_step(stream, s):
        i, kind, way, n = stream
        off = (way * (n + 1 - s)) % 8
        o = turn(y, off, 8)
        arrive(off)
        total = part[c, o, i] + sib[o, i]
        if s > 1:
            ring_copy(stream, s - 1).wait_recv()
            total = total + ring[i, kind, s - 2]
        part[c, o, i] = total
        ring_copy(stream, s).start()

    product(0)
    pl.semaphore_wait(barrier, jnp.where(active, 48, 17))
    pass_on(0)
    small_copy.start()
    product(1)
    pass_on(1)
    ring_step(STREAMS[0], 1)
    ring_step(STREAMS[1], 1)
    product(2)
    pass_on(2)
    ring_step(STREAMS[2], 1)
    product(3)
    pass_on(3)
    ring_step(STREAMS[3], 1)
    for s in range(2, 5):
        for stream in STREAMS:
            if s <= stream[3]:
                ring_step(stream, s)

    arrive(0)

    def z_copy(i):
        return send(part.at[c, y, i], zrecv.at[z], z_ss.at[i], z_rs.at[z], dev(2 * c + i, y, c, m))

    for i in range(2):
        ring_copy(STREAMS[i], 4).wait_recv()
        ring_copy(STREAMS[2 + i], 3).wait_recv()
        total = part[c, y, i] + sib[y, i] + ring[i, 0, 3] + ring[i, 1, 2]

        @pl.when(z != 2 * c + i)
        def _():
            part[c, y, i] = total
            z_copy(i).start()

        @pl.when(z == 2 * c + i)
        def _():
            zrecv[z] = total

    small_copy.wait_recv()

    def first_copy(dz, dm):
        zz = turn(z, dz, 4)
        mm = turn(m, dm, 8)
        rows = pl.ds(0, 16) if dm == 0 else pl.ds(8, 8)
        n = dz * 8 + dm
        slot = z * 8 + m
        return send(
            m1.at[rows], p1.at[slot, rows], p1_ss.at[n], p1_rs.at[slot], dev(zz, y, zz // 2, mm)
        )

    def first_wait(dz, dm):
        zz = turn(z, dz, 4)
        mm = turn(m, dm, 8)
        rows = pl.ds(0, 16) if dm == 0 else pl.ds(8, 8)
        slot = zz * 8 + mm
        send(m1.at[rows], p1.at[slot, rows], p1_ss.at[dz * 8 + dm], p1_rs.at[slot], dev(zz, y, zz // 2, mm)).wait_recv()

    def gather_copy(dk):
        k = turn(2 * q + c, dk, 8)
        return send(
            spread.at[pl.ds(pl.multiple_of(k * SPREAD, SPREAD), SPREAD)],
            gathered.at[q],
            g_ss.at[dk],
            g_rs.at[q],
            dev(z, 4 * h + k // 2, lax.rem(k, 2), m),
        )

    def second_copy(dy, cc):
        return send(
            m2, p2.at[y], p2_ss.at[dy * 2 + cc], p2_rs.at[y],
            dev(z, turn(y, dy, 8), lax.rem(c + cc, 2), m),
        )

    first_order = [(dz, dm) for dm in (6, 5, 7, 2, 4, 1, 3, 0) for dz in (2, 1, 3, 0) if dz or dm]
    second_order = [(dy, cc) for dy in (4, 3, 5, 2, 6, 1, 7, 0) for cc in (0, 1) if dy or cc]

    @pl.when(active)
    def _():
        for dz in range(1, 4):
            zz = turn(z, dz, 4)
            send(part.at[c, y, 0], zrecv.at[zz], z_ss.at[0], z_rs.at[zz], dev(zz, y, c, m)).wait_recv()
        column = [None] * LANE_TILES
        rows = [None] * 3
        for j in range(3):
            for lb in range(LANE_TILES):
                t = j * LANE_TILES + lb
                at = slice(t * 8, t * 8 + 8)
                g = (zrecv[0, at] + zrecv[1, at]) + (zrecv[2, at] + zrecv[3, at])
                spread[pl.ds(t, 8, stride=SPREAD), :] = g
                square = g * g + eps_sq
                column[lb] = square if j == 0 else column[lb] + square
                rows[j] = square if lb == 0 else rows[j] + square
        for lb in range(LANE_TILES):
            m1[lb : lb + 1, :] = jnp.sum(column[lb], axis=0, keepdims=True)
        every = jnp.sum(rows[0] + rows[1] + rows[2], axis=0, keepdims=True)
        m1[9:10, :] = jnp.broadcast_to(jnp.sum(every, axis=1, keepdims=True), (1, 128))
        m1[10:12, :] = small[2:4, :] + small_recv[2:4, :]
        for j in range(3):
            each = jnp.broadcast_to(jnp.sum(rows[j], axis=1, keepdims=True), (8, 128))
            m1[12 + j : 13 + j, :] = jnp.sum(jnp.where(lane8 == sub8, each, 0.0), axis=0, keepdims=True)
        m1[15:16, :] = jnp.zeros((1, 128), F32)
        for dz, dm in first_order:
            first_copy(dz, dm).start()
        for dk in range(1, 8):
            gather_copy(dk).start()
        gathered[q] = spread[pl.ds(pl.multiple_of((2 * q + c) * SPREAD, SPREAD), SPREAD), :]
        own = m1[8:16, :]
        same_m, same_z, other = own, own, jnp.zeros((8, 128), F32)
        same_m_top = m1[0:8, :]
        for dz, dm in reversed(first_order):
            first_wait(dz, dm)
            slot = turn(z, dz, 4) * 8 + turn(m, dm, 8)
            tile = p1[slot, 8:16, :]
            if dm == 0:
                same_m = same_m + tile
                same_m_top = same_m_top + p1[slot, 0:8, :]
            elif dz == 0:
                same_z = same_z + tile
            else:
                other = other + tile
        everyone = same_m + same_z - own + other
        m2[0:8, :] = same_m_top
        m2[8:16, :] = jnp.where(sub8 == 0, same_m, jnp.where(sub8 < 4, everyone, same_z))
        for dy, cc in second_order:
            second_copy(dy, cc).start()
        p2[y] = m2[...]

    for dy in range(8):
        yy = turn(y, dy, 8)
        landed = send(m2, p2.at[yy], p2_ss.at[0], p2_rs.at[yy], dev(z, yy, 1 - c, m))
        if dy == 0:

            @pl.when(jnp.logical_not(active))
            def _():
                landed.wait_recv()
        else:
            landed.wait_recv()
    for dq in range(4):
        qq = turn(q, dq, 4)
        landed = send(
            spread.at[pl.ds(0, SPREAD)], gathered.at[qq], g_ss.at[0], g_rs.at[qq], dev(z, 4 * h + qq, 1 - c, m)
        )
        if dq == 0:

            @pl.when(jnp.logical_not(active))
            def _():
                landed.wait_recv()
        else:
            landed.wait_recv()

    for qq in range(4):
        out_ref[qq * SPREAD : (qq + 1) * SPREAD, :] = gathered[qq]
        out_ref[GATHERED + qq * 16 : GATHERED + qq * 16 + 16, :] = p2[qq] + p2[4 + qq]
    all_y = p2[0, 8:16, :]
    for yy in range(1, 8):
        all_y = all_y + p2[yy, 8:16, :]
    same_h = p2[4 * h, 8:16, :]
    for qq in range(1, 4):
        same_h = same_h + p2[4 * h + qq, 8:16, :]
    mine = jnp.sum(jnp.where(lane8 == 2 * q + c, same_h, 0.0), axis=1, keepdims=True)
    out_ref[SUMS : SUMS + 8, :] = jnp.where(sub8 < 4, all_y, jnp.broadcast_to(mine, (8, 128)))

    for o in range(8):
        sib_copy(o).wait_send()
    small_copy.wait_send()
    for stream in STREAMS:
        for s in range(1, stream[3] + 1):
            ring_copy(stream, s).wait_send()
    for i in range(2):

        @pl.when(z != 2 * c + i)
        def _():
            z_copy(i).wait_send()

    @pl.when(active)
    def _():
        for dz, dm in first_order:
            first_copy(dz, dm).wait_send()
        for dk in range(1, 8):
            gather_copy(dk).wait_send()
        for dy, cc in second_order:
            second_copy(dy, cc).wait_send()


def finish_kernel(
    sums_ref, matrix_ref, momentum_ref, row_factor_ref, row_rest_ref, col_factor_ref, col_rest_ref,
    new_matrix_ref, new_momentum_ref, new_row_ref, new_col_ref,
):
    entries = float(ROWS) * float(BLOCK_COLS)
    total = sums_ref[SUMS + 1 : SUMS + 2, :]
    matrix_sq = sums_ref[SUMS + 2 : SUMS + 3, :]
    base = sums_ref[SUMS + 3 : SUMS + 4, :] * 0.125
    row_mean = (base + (1.0 - beta_two) * (total / FULL_COLS)) / ROWS
    step = (1.0 - beta_one) * rel_step * jnp.sqrt(matrix_sq / entries)
    row_sums = sums_ref[SUMS + 4 : SUMS + 7, :]
    sub = lax.broadcasted_iota(jnp.int32, (3, 128), 0)

    def down(ref):
        return jnp.where(sub == 0, ref[0], jnp.where(sub == 1, ref[1], ref[2]))

    new_row = beta_two * down(row_factor_ref) + (1.0 - beta_two) * ((row_sums + down(row_rest_ref)) / FULL_COLS)
    for j in range(3):
        new_row_ref[j] = new_row[j, 0]
    row_scale = lax.rsqrt(new_row / row_mean) * step
    for qq in range(4):
        at = slice(qq * LANE_TILES, (qq + 1) * LANE_TILES)
        column_sum = sums_ref[GATHERED + qq * 16 : GATHERED + qq * 16 + LANE_TILES, :]
        new_col = beta_two * col_factor_ref[at, :] + (1.0 - beta_two) * (
            (column_sum + col_rest_ref[at, :]) / FULL_ROWS
        )
        new_col_ref[at, :] = new_col
        inverse_col = lax.rsqrt(new_col)
        for lb in range(LANE_TILES):
            b = (qq * LANE_TILES + lb) * 128
            g = sums_ref[pl.ds(qq * SPREAD + lb, 3, stride=LANE_TILES), :]
            change = g * row_scale * inverse_col[lb : lb + 1, :]
            new_momentum = beta_one * momentum_ref[:, b : b + 128] + change
            new_momentum_ref[:, b : b + 128] = new_momentum
            new_matrix_ref[:, b : b + 128] = matrix_ref[:, b : b + 128] - new_momentum


def on_device(inputs, cotangent, matrix, momentum, row_factor, col_factor, row_rest, col_rest):
    vmem = pl.BlockSpec(memory_space=VMEM)
    smem = pl.BlockSpec(memory_space=pltpu.SMEM)
    hbm = pl.BlockSpec(memory_space=pl.ANY)
    dma = pltpu.SemaphoreType.DMA
    sums = pl.pallas_call(
        reduce_kernel,
        out_shape=jax.ShapeDtypeStruct((SUMS + 8, 128), F32),
        in_specs=[hbm, hbm, vmem, smem, smem],
        out_specs=vmem,
        scratch_shapes=[
            VMEM((ROWS, 480), jnp.bfloat16),
            VMEM((ROWS, 480), jnp.bfloat16),
            VMEM((4, 480, GROUP), jnp.bfloat16),
            VMEM((2, 8, 2, CHUNK, 128), F32),
            VMEM((8, 2, CHUNK, 128), F32),
            VMEM((2, 2, 4, CHUNK, 128), F32),
            VMEM((4, CHUNK, 128), F32),
            VMEM((8 * SPREAD, 128), F32),
            VMEM((4, SPREAD, 128), F32),
            VMEM((8, 128), F32),
            VMEM((8, 128), F32),
            VMEM((16, 128), F32),
            VMEM((32, 16, 128), F32),
            VMEM((16, 128), F32),
            VMEM((8, 16, 128), F32),
            dma, dma((4,)), dma((8,)), dma((8,)), dma, dma,
            dma((2, 2, 4)), dma((2, 2, 4)), dma((2,)), dma((4,)), dma((8,)), dma((4,)),
            dma((32,)), dma((32,)), dma((16,)), dma((8,)),
        ],
        compiler_params=pltpu.CompilerParams(
            collective_id=0, has_side_effects=True, vmem_limit_bytes=40 * 1024 * 1024
        ),
        name="reduce",
    )(inputs.T, cotangent, matrix, row_factor, row_rest)
    new_matrix, new_momentum, new_row, new_col = pl.pallas_call(
        finish_kernel,
        out_shape=(
            jax.ShapeDtypeStruct(matrix.shape, F32),
            jax.ShapeDtypeStruct(matrix.shape, F32),
            jax.ShapeDtypeStruct((3,), F32),
            jax.ShapeDtypeStruct((36, 128), F32),
        ),
        in_specs=[vmem, vmem, vmem, smem, smem, vmem, vmem],
        out_specs=(vmem, vmem, smem, vmem),
        name="finish",
    )(sums, matrix, momentum, row_factor, row_rest, col_factor.reshape(36, 128), col_rest.reshape(36, 128))
    return (new_matrix, new_momentum, new_row, new_col.reshape(4608))


def solution(mesh):
    placed = (
        P("dp", None),
        P("dp", "mp"),
        P("dp", "mp"),
        P("dp", "mp"),
        P("dp"),
        P("mp"),
        P("dp"),
        P("mp"),
    )
    return jax.shard_map(
        on_device,
        mesh=mesh,
        in_specs=placed,
        out_specs=(P("dp", "mp"), P("dp", "mp"), P("dp"), P("mp")),
        check_vma=False,
    )
```

time: 869 us -> 65.6 us (0.08)
  waiting for transfers between devices: 436 us -> 0 us
  blocking collectives: 404 us -> 0 us
  Pallas kernels: 0 us -> 58.7 us
  between operations: 16.1 us -> 0.66 us
    unnamed x2 -> x0, waiting for transfers between devices: 436 us -> none
    psum x3 -> x0, blocking collectives: 404 us -> none  [the longest x1 269 us: on_device(): column_sum = lax.psum(jnp.sum(squares, axis=0), 'dp')]
    pallas_call x0 -> x2, Pallas kernels: none -> 58.7 us  [the longest x1 56.9 us: on_device(): pl.pallas_call(reduce_kernel, out_shape=jax.ShapeDtypeStruct((SUMS + 8, 1...]
  transfers between devices with their start and end apart: 1 -> 0, of which waited for: 1 -> 0; matrix products, arithmetic and copies ran while one was open for 0% -> 0% of each run, Pallas kernels for 0% -> 0%
where the time goes in v1:
time: 65.6 us; the launch traced here: 65.3 us
  Pallas kernels  58.7 us (89%)
  local copies, waits for them, and re-layouts  6 us (9%)
  between operations  0.66 us (1%)
    pallas_call x1, Pallas kernels, on_device(): pl.pallas_call(reduce_kernel, out_shape=jax.ShapeDtypeStruct((SUMS + 8, 1...  56.9 us
    unnamed x12, local copies, waits for them, and re-layouts  6 us
    pallas_call x1, Pallas kernels, on_device(): pl.pallas_call(finish_kernel, out_shape=(jax.ShapeDtypeStruct(matrix.shap...  1.74 us

profile of v1, /device:TPU:1, one launch (start us, length us, event | category | flops | bytes accessed | tf_op | source)
XLA Modules:
  0.0 65.3 jit_solution(10314590607185511035)
XLA Ops:
  0.6 0.0 copy-start
  0.6 2.2 %copy-done = bf16[480,4608]{1,0:T(8,128)(2,1)S(1)} copy-done((bf16[480,4608]{1,0:T(8,128)(2,1)S(1)}, bf16[480,4608]{1,0:T(8,128)(2,1)}, u32[]{:S(2)}) %copy-start) | copy-done | bytes 4423704
  2.9 0.0 copy-start.2
  2.9 0.9 %copy-done.2 = f32[3,4608]{1,0:T(4,128)S(1)} copy-done((f32[3,4608]{1,0:T(4,128)S(1)}, f32[3,4608]{1,0:T(4,128)}, u32[]{:S(2)}) %copy-start.2) | copy-done | bytes 55320
  3.8 0.0 copy-start.3
  3.8 0.9 %copy-done.3 = bf16[480,192]{0,1:T(8,128)(2,1)S(1)} copy-done((bf16[480,192]{0,1:T(8,128)(2,1)S(1)}, bf16[480,192]{0,1:T(8,128)(2,1)}, u32[]{:S(2)}) %copy-start.3) | copy-done | bytes 184344
  4.7 0.0 copy-start.4
  4.7 0.7 copy-done.4
  5.4 0.0 copy-start.5
  5.4 0.7 copy-done.5
  6.0 56.9 %reduce.1.sums_ref = f32[200,128]{1,0:T(8,128)S(1)} custom-call(bf16[192,480]{1,0:T(8,128)(2,1)S(1)} %bitcast.4, bf16[480,4608]{1,0:T(8,128)(2,1)S(1)} %copy-done, f32[3,4608]{1,0:T(4,128)S(1)} %copy-done.2, f32[3]{0:T(128)S(1)} %copy-done.4, f32[3]{0:T(128)S(1)} %copy-done.5), custom_call_target="tpu_custom_call" | custom-call | tf_op jit(solution)/shard_map/reduce/pallas_call | solution.py:400
  63.0 0.0 copy-start.1
  63.0 0.6 copy-done.1
  63.6 1.7 %finish.1 = (f32[3,4608]{1,0:T(4,128)}, f32[3,4608]{1,0:T(4,128)}, f32[3]{0:T(128)}, f32[36,128]{1,0:T(8,128)}) custom-call(f32[200,128]{1,0:T(8,128)} %copy-done.1, f32[3,4608]{1,0:T(4,128)} %matrix_ref.3, f32[3,4608]{1,0:T(4,128)} %momentum_ref.1, f32[3]{0:T(128)} %row_factor_ref.3, f32[3]{0:T(128)} %row_rest_ref.3, f32[36,128]{1,0:T(8,128)} %bitcast.5, ...), custom_call_target="tpu_custom_call" | custom-call | tf_op jit(solution)/shard_map/finish/pallas_call | solution.py:430
Async XLA Ops:
  0.6 2.3 %copy-start = (bf16[480,4608]{1,0:T(8,128)(2,1)S(1)}, bf16[480,4608]{1,0:T(8,128)(2,1)}, u32[]{:S(2)}) copy-start(bf16[480,4608]{1,0:T(8,128)(2,1)} %cot_hbm.1) | copy-start | bytes 13271044
  2.9 0.9 %copy-start.2 = (f32[3,4608]{1,0:T(4,128)S(1)}, f32[3,4608]{1,0:T(4,128)}, u32[]{:S(2)}) copy-start(f32[3,4608]{1,0:T(4,128)} %matrix_ref.3) | copy-start | bytes 165892
  3.8 0.9 %copy-start.3 = (bf16[480,192]{0,1:T(8,128)(2,1)S(1)}, bf16[480,192]{0,1:T(8,128)(2,1)}, u32[]{:S(2)}) copy-start(bf16[480,192]{0,1:T(8,128)(2,1)} %param.8) | copy-start | bytes 552964
  4.7 0.7 %copy-start.4 = (f32[3]{0:T(128)S(1)}, f32[3]{0:T(128)}, u32[]{:S(2)}) copy-start(f32[3]{0:T(128)} %row_factor_ref.3) | copy-start | bytes 40
  5.4 0.7 %copy-start.5 = (f32[3]{0:T(128)S(1)}, f32[3]{0:T(128)}, u32[]{:S(2)}) copy-start(f32[3]{0:T(128)} %row_rest_ref.3) | copy-start | bytes 40
  63.0 0.6 copy-start.1

commit v2 on v1

v2 whole, which is shorter than its diff:
```python
import functools

import jax
import jax.numpy as jnp
from jax import lax
from jax.experimental import pallas as pl
from jax.experimental.pallas import tpu as pltpu
from jax.sharding import PartitionSpec as P

FULL_ROWS = 18432
FULL_COLS = 73728
ROWS = 192
BLOCK_COLS = 36864

beta_two = 1.0 - 10.0 ** (-0.8)
beta_one = 0.9
rel_step = 0.01
eps_sq = 1e-30

MESH = pl.DeviceIdType.MESH
F32 = jnp.float32
VMEM = pltpu.VMEM

LANE_TILES = 9
A_LANES = 6
A_ROWS = A_LANES * 24
B_ROWS = (LANE_TILES - A_LANES) * 24
GROUP = LANE_TILES * 128
SPREAD = 32
STREAMS = ((0, 0, 1, 4), (1, 0, -1, 4), (0, 1, -1, 3), (1, 1, 1, 3))
GROUP_ORDER = (0, 1, 3, 2)
GATHERED = 4 * SPREAD
SUMS = GATHERED + 4 * 16
FIRST_ORDER = tuple((dz, dm) for dm in (6, 5, 7, 2, 4, 1, 3, 0) for dz in (2, 1, 3, 0) if dz or dm)
SECOND_ORDER = tuple((dy, cc) for dy in (4, 3, 5, 2, 6, 1, 7, 0) for cc in (0, 1) if dy or cc)

GATHER_ORDER = ((2, 0), (2, 1), (1, 0), (1, 1), (3, 0), (3, 1), (0, 1))
Y_AT = 5


def slot_of(dz, dm):
    if dm == 0:
        return pl.ds((dz - 1) * 16, 16)
    return pl.ds(48 + (dz * 7 + dm - 1) * 8, 8)


def send(src, dst, send_sem, recv_sem, target):
    return pltpu.make_async_remote_copy(
        src_ref=src, dst_ref=dst, send_sem=send_sem, recv_sem=recv_sem, device_id=target, device_id_type=MESH
    )


def landed(ref, sem):
    pltpu.make_async_copy(ref, ref, sem).wait()


def reduce_kernel(
    inputs_hbm, cot_hbm, matrix_hbm, row_factor_hbm, row_rest_hbm, out_ref,
    inp, matrix_ref, row_factor_ref, row_rest_ref, lhs, cot, part, sib, qpart, qsib, ring, zrecv, zq, yq,
    spread, gathered, small, small_recv, m1, p1, m2, p2,
    in_sem, late_sem, cot_sem, sib_ss, sib_rs, qsib_ss, qsib_rs, small_ss, small_rs, ring_ss, ring_rs,
    z_ss, z_rs, zq_ss, zq_rs, yq_ss, yq_rs, g_ss, g_rs, g_own, p1_ss, p1_rs, p2_ss, p2_rs, p2_own,
):
    d = lax.axis_index("dp")
    m = lax.axis_index("mp")
    z = d // 16
    y = lax.rem(d // 2, 8)
    c = lax.rem(d, 2)
    h = y // 4
    q = lax.rem(y, 4)
    home = z // 2
    active = c == home

    def dev(zz, yy, cc, mm):
        return (zz * 16 + yy * 2 + cc, mm)

    def turn(v, k, n):
        return lax.rem(v + k + n, n)

    in_copy = pltpu.make_async_copy(inputs_hbm, inp, in_sem)
    in_copy.start()
    late_copies = []
    for n, (src, dst) in enumerate(
        ((matrix_hbm, matrix_ref), (row_factor_hbm, row_factor_ref), (row_rest_hbm, row_rest_ref))
    ):
        late_copies.append(pltpu.make_async_copy(src, dst, late_sem.at[n]))
    cot_copies = []
    for n, off in enumerate(GROUP_ORDER):
        g = turn(q, off, 4)
        copy = pltpu.make_async_copy(
            cot_hbm.at[:, pl.ds(pl.multiple_of(g * GROUP, 128), GROUP)], cot.at[n], cot_sem.at[n]
        )
        cot_copies.append(copy)
    cot_copies[0].start()

    barrier = pltpu.get_barrier_semaphore()

    def hello(target):
        pl.semaphore_signal(barrier, inc=1, device_id=target, device_id_type=MESH)

    @pl.when(active)
    def _():
        for dz, dm in FIRST_ORDER:
            zz = turn(z, dz, 4)
            hello(dev(zz, y, zz // 2, turn(m, dm, 8)))
        for i in range(2):
            hello(dev((1 - home) * 2 + i, y, c, m))

    @pl.when(jnp.logical_not(active))
    def _():
        for i in range(2):
            hello(dev(2 * c + i, y, c, m))

    for dy, cc in SECOND_ORDER:
        hello(dev(z, turn(y, dy, 8), lax.rem(c + cc, 2), m))

    row = lax.broadcasted_iota(jnp.int32, (ROWS, ROWS), 0)
    col = lax.broadcasted_iota(jnp.int32, (ROWS, ROWS), 1)
    block = (row * 2731) >> 16
    inner = row - block * 24
    want = block * 24 + 3 * (inner & 7) + (inner >> 3)
    pick = jnp.where(col == want, 1.0, 0.0).astype(jnp.bfloat16)
    in_copy.wait()
    cot_copies[1].start()
    lhs[...] = jnp.dot(pick, inp[...], preferred_element_type=F32).astype(jnp.bfloat16)

    sub8 = lax.broadcasted_iota(jnp.int32, (8, 128), 0)
    lane8 = lax.broadcasted_iota(jnp.int32, (8, 128), 1)

    def product(n):
        cot_copies[n].wait()
        if n < 2:
            cot_copies[n + 2].start()
        if n == 2:
            for copy in late_copies:
                copy.start()
        g = turn(q, GROUP_ORDER[n], 4)
        acc = jnp.dot(lhs[...], cot[n], preferred_element_type=F32)
        for zh in range(2):
            for i in range(2):
                for hh in range(2):
                    r0 = ((zh * 2 + i) * 2 + hh) * 24
                    for lb in range(LANE_TILES):
                        for j in range(3):
                            tile = acc[r0 + j * 8 : r0 + j * 8 + 8, lb * 128 : lb * 128 + 128]
                            if lb < A_LANES:
                                t = (lb * 3 + j) * 8
                                part[zh, hh * 4 + g, i, t : t + 8, :] = tile
                            else:
                                t = ((lb - A_LANES) * 3 + j) * 8
                                qpart[zh, g, i, hh, t : t + 8, :] = tile

    sibling = dev(z, y, 1 - c, m)

    def sib_copy(o):
        return send(part.at[1 - c, o], sib.at[o], sib_ss, sib_rs.at[o], sibling)

    def qsib_copy(g):
        return send(qpart.at[1 - c, g], qsib.at[g], qsib_ss, qsib_rs.at[g], sibling)

    small_copy = send(small, small_recv, small_ss, small_rs, sibling)

    def pass_on(n):
        for off in (4, 0):
            sib_copy(turn(y, GROUP_ORDER[n] + off, 8)).start()
        qsib_copy(turn(q, GROUP_ORDER[n], 4)).start()

    def zq_copy(g, i):
        return send(qpart.at[c, g, i], zq.at[z, g], zq_ss.at[i], zq_rs, dev(2 * c + i, y, c, m))

    def along_z(n):
        g = turn(q, GROUP_ORDER[n], 4)
        qsib_copy(g).wait_recv()
        for i in range(2):
            qpart[c, g, i] = qpart[c, g, i] + qsib[g, i]

            @pl.when(z != 2 * c + i)
            def _():
                zq_copy(g, i).start()

    arrived = set()

    def arrive(k):
        k %= 8
        if k not in arrived:
            arrived.add(k)
            sib_copy(turn(y, k, 8)).wait_recv()

    def ring_copy(stream, s):
        i, kind, way, n = stream
        o = turn(y, (way * (n + 1 - s)) % 8, 8)
        return send(
            part.at[c, o, i],
            ring.at[(i * 2 + kind) * 4 + s - 1],
            ring_ss,
            ring_rs.at[i, kind, s - 1],
            dev(z, turn(y, way % 8, 8), c, m),
        )

    def ring_step(stream, s):
        i, kind, way, n = stream
        off = (way * (n + 1 - s)) % 8
        o = turn(y, off, 8)
        arrive(off)
        total = part[c, o, i] + sib[o, i]
        if s > 1:
            ring_copy(stream, s - 1).wait_recv()
            total = total + ring[(i * 2 + kind) * 4 + s - 2]
        part[c, o, i] = total
        ring_copy(stream, s).start()

    product(0)
    pl.semaphore_wait(barrier, jnp.where(active, 48, 17))
    pass_on(0)
    product(1)
    pass_on(1)
    ring_step(STREAMS[0], 1)
    ring_step(STREAMS[1], 1)
    product(2)
    pass_on(2)
    ring_step(STREAMS[2], 1)
    along_z(0)
    product(3)
    pass_on(3)
    ring_step(STREAMS[3], 1)
    for n in (1, 2, 3):
        along_z(n)

    for copy in late_copies:
        copy.wait()
    mat = matrix_ref[...]
    msq = jnp.sum(jnp.sum(mat * mat, axis=0, keepdims=True), axis=1, keepdims=True)
    base = jnp.float32(0.0)
    for j in range(3):
        base = base + beta_two * row_factor_ref[j] + (1.0 - beta_two) * (row_rest_ref[j] * (1.0 / FULL_COLS))
    small[...] = jnp.where(sub8 == 2, msq, jnp.where(sub8 == 3, base, 0.0))

    small_copy.start()

    def yq_copy(g, hh):
        return send(
            qpart.at[c, g, z - 2 * home, hh], yq.at[y], yq_ss, yq_rs, dev(z, 4 * hh + g, c, m)
        )

    def along_y():
        @pl.when(active)
        def _():
            landed(zq.at[pl.ds(0, 3)], zq_rs)
            for dy in (4, 3, 5, 2, 6, 1, 7, 0):
                yy = turn(y, dy, 8)
                g, hh = lax.rem(yy, 4), yy // 4
                total = qpart[c, g, z - 2 * home, hh]
                for dz in range(1, 4):
                    total = total + zq[turn(z, dz, 4), g, hh]
                if dy:
                    qpart[c, g, z - 2 * home, hh] = total
                    yq_copy(g, hh).start()
                else:
                    yq[y] = total

    for s in range(2, 5):
        if s == Y_AT:
            along_y()
        for stream in STREAMS:
            if s <= stream[3]:
                ring_step(stream, s)
    if Y_AT > 4:
        along_y()

    arrive(0)

    def z_copy(i):
        return send(part.at[c, y, i], zrecv.at[z], z_ss.at[i], z_rs, dev(2 * c + i, y, c, m))

    for i in range(2):
        ring_copy(STREAMS[2 + i], 3).wait_recv()
        ring_copy(STREAMS[i], 4).wait_recv()
        total = part[c, y, i] + sib[y, i] + ring[i * 8 + 3] + ring[i * 8 + 6]

        @pl.when(z != 2 * c + i)
        def _():
            part[c, y, i] = total
            z_copy(i).start()

        @pl.when(z == 2 * c + i)
        def _():
            zrecv[z] = total

    small_copy.wait_recv()

    def first_copy(dz, dm):
        zz = turn(z, dz, 4)
        rows = pl.ds(0, 16) if dm == 0 else pl.ds(8, 8)
        slot = slot_of((4 - dz) % 4, (8 - dm) % 8)
        return send(m1.at[rows], p1.at[slot], p1_ss, p1_rs, dev(zz, y, zz // 2, turn(m, dm, 8)))

    def gather_copy(dq, cc):
        k = 2 * turn(q, dq, 4) + lax.rem(c + cc, 2)
        return send(
            spread.at[pl.ds(pl.multiple_of(k * SPREAD, SPREAD), SPREAD)],
            gathered.at[q],
            g_ss,
            g_rs if dq else g_own,
            dev(z, 4 * h + turn(q, dq, 4), lax.rem(c + cc, 2), m),
        )

    def second_copy(dy, cc):
        return send(
            m2, p2.at[y], p2_ss, p2_rs if dy else p2_own, dev(z, turn(y, dy, 8), lax.rem(c + cc, 2), m)
        )

    @pl.when(active)
    def _():
        landed(yq.at[pl.ds(0, 7)], yq_rs)
        landed(zrecv.at[pl.ds(0, 3)], z_rs)
        column = [None] * LANE_TILES
        rows = [None] * 3
        for lb in range(LANE_TILES):
            for j in range(3):
                if lb < A_LANES:
                    t = (lb * 3 + j) * 8
                    at = slice(t, t + 8)
                    g = (zrecv[0, at] + zrecv[1, at]) + (zrecv[2, at] + zrecv[3, at])
                else:
                    t = ((lb - A_LANES) * 3 + j) * 8
                    at = slice(t, t + 8)
                    g = ((yq[0, at] + yq[1, at]) + (yq[2, at] + yq[3, at])) + (
                        (yq[4, at] + yq[5, at]) + (yq[6, at] + yq[7, at])
                    )
                spread[pl.ds(j * LANE_TILES + lb, 8, stride=SPREAD), :] = g
                square = g * g + eps_sq
                column[lb] = square if j == 0 else column[lb] + square
                rows[j] = square if lb == 0 else rows[j] + square
        for lb in range(LANE_TILES):
            m1[lb : lb + 1, :] = jnp.sum(column[lb], axis=0, keepdims=True)
        every = jnp.sum(rows[0] + rows[1] + rows[2], axis=0, keepdims=True)
        m1[9:10, :] = jnp.broadcast_to(jnp.sum(every, axis=1, keepdims=True), (1, 128))
        m1[10:12, :] = small[2:4, :] + small_recv[2:4, :]
        for j in range(3):
            each = jnp.broadcast_to(jnp.sum(rows[j], axis=1, keepdims=True), (8, 128))
            m1[12 + j : 13 + j, :] = jnp.sum(jnp.where(lane8 == sub8, each, 0.0), axis=0, keepdims=True)
        m1[15:16, :] = jnp.zeros((1, 128), F32)
        for dz, dm in FIRST_ORDER:
            first_copy(dz, dm).start()
        for dq, cc in GATHER_ORDER:
            gather_copy(dq, cc).start()
        gathered[q] = spread[pl.ds(pl.multiple_of((2 * q + c) * SPREAD, SPREAD), SPREAD), :]

    landed(sib, sib_ss)
    landed(qsib, qsib_ss)
    small_copy.wait_send()
    landed(ring.at[pl.ds(0, 14)], ring_ss)
    for i in range(2):

        @pl.when(z != 2 * c + i)
        def _():
            z_copy(i).wait_send()
            landed(zq.at[0], zq_ss.at[i])

    @pl.when(active)
    def _():
        landed(yq.at[pl.ds(0, 7)], yq_ss)
        landed(p1, p1_ss)
        own = m1[8:16, :]
        same_m, same_z, other = own, own, jnp.zeros((8, 128), F32)
        same_m_top = m1[0:8, :]
        landed(p1, p1_rs)
        for dz, dm in FIRST_ORDER:
            tile = slot_of(dz, dm)
            if dm == 0:
                both = p1[tile, :]
                same_m = same_m + both[8:16, :]
                same_m_top = same_m_top + both[0:8, :]
            elif dz == 0:
                same_z = same_z + p1[tile, :]
            else:
                other = other + p1[tile, :]
        everyone = same_m + same_z - own + other
        m2[0:8, :] = same_m_top
        m2[8:16, :] = jnp.where(sub8 == 0, same_m, jnp.where(sub8 < 4, everyone, same_z))
        for dy, cc in SECOND_ORDER:
            second_copy(dy, cc).start()
        p2[y] = m2[...]
        landed(spread.at[pl.ds(0, 7 * SPREAD)], g_ss)
        landed(spread.at[pl.ds(0, 15 * 16)], p2_ss)

    landed(gathered.at[pl.ds(0, 3)], g_rs)

    @pl.when(jnp.logical_not(active))
    def _():
        landed(gathered.at[0], g_own)
        landed(p2.at[0], p2_own)

    landed(p2.at[pl.ds(0, 7)], p2_rs)
    for qq in range(4):
        out_ref[qq * SPREAD : (qq + 1) * SPREAD, :] = gathered[qq]
        out_ref[GATHERED + qq * 16 : GATHERED + qq * 16 + 16, :] = p2[qq] + p2[4 + qq]
    all_y = p2[0, 8:16, :]
    for yy in range(1, 8):
        all_y = all_y + p2[yy, 8:16, :]
    same_h = p2[4 * h, 8:16, :]
    for qq in range(1, 4):
        same_h = same_h + p2[4 * h + qq, 8:16, :]
    mine = jnp.sum(jnp.where(lane8 == 2 * q + c, same_h, 0.0), axis=1, keepdims=True)
    out_ref[SUMS : SUMS + 8, :] = jnp.where(sub8 < 4, all_y, jnp.broadcast_to(mine, (8, 128)))


def finish_kernel(
    sums_ref, matrix_ref, momentum_ref, row_factor_ref, row_rest_ref, col_factor_ref, col_rest_ref,
    new_matrix_ref, new_momentum_ref, new_row_ref, new_col_ref,
):
    entries = float(ROWS) * float(BLOCK_COLS)
    total = sums_ref[SUMS + 1 : SUMS + 2, :]
    matrix_sq = sums_ref[SUMS + 2 : SUMS + 3, :]
    base = sums_ref[SUMS + 3 : SUMS + 4, :] * 0.125
    row_mean = (base + (1.0 - beta_two) * (total / FULL_COLS)) / ROWS
    step = (1.0 - beta_one) * rel_step * jnp.sqrt(matrix_sq / entries)
    row_sums = sums_ref[SUMS + 4 : SUMS + 7, :]
    sub = lax.broadcasted_iota(jnp.int32, (3, 128), 0)

    def down(ref):
        return jnp.where(sub == 0, ref[0], jnp.where(sub == 1, ref[1], ref[2]))

    new_row = beta_two * down(row_factor_ref) + (1.0 - beta_two) * ((row_sums + down(row_rest_ref)) / FULL_COLS)
    for j in range(3):
        new_row_ref[j] = new_row[j, 0]
    row_scale = lax.rsqrt(new_row / row_mean) * step
    for qq in range(4):
        at = slice(qq * LANE_TILES, (qq + 1) * LANE_TILES)
        column_sum = sums_ref[GATHERED + qq * 16 : GATHERED + qq * 16 + LANE_TILES, :]
        new_col = beta_two * col_factor_ref[at, :] + (1.0 - beta_two) * (
            (column_sum + col_rest_ref[at, :]) / FULL_ROWS
        )
        new_col_ref[at, :] = new_col
        inverse_col = lax.rsqrt(new_col)
        for lb in range(LANE_TILES):
            b = (qq * LANE_TILES + lb) * 128
            g = sums_ref[pl.ds(qq * SPREAD + lb, 3, stride=LANE_TILES), :]
            change = g * row_scale * inverse_col[lb : lb + 1, :]
            new_momentum = beta_one * momentum_ref[:, b : b + 128] + change
            new_momentum_ref[:, b : b + 128] = new_momentum
            new_matrix_ref[:, b : b + 128] = matrix_ref[:, b : b + 128] - new_momentum


def on_device(inputs, cotangent, matrix, momentum, row_factor, col_factor, row_rest, col_rest):
    vmem = pl.BlockSpec(memory_space=VMEM)
    smem = pl.BlockSpec(memory_space=pltpu.SMEM)
    hbm = pl.BlockSpec(memory_space=pltpu.HBM)
    dma = pltpu.SemaphoreType.DMA
    sums = pl.pallas_call(
        reduce_kernel,
        out_shape=jax.ShapeDtypeStruct((SUMS + 8, 128), F32),
        in_specs=[hbm] * 5,
        out_specs=vmem,
        scratch_shapes=[
            VMEM((ROWS, 480), jnp.bfloat16),
            VMEM((3, 4608), F32),
            pltpu.SMEM((3,), F32),
            pltpu.SMEM((3,), F32),
            VMEM((ROWS, 480), jnp.bfloat16),
            VMEM((4, 480, GROUP), jnp.bfloat16),
            VMEM((2, 8, 2, A_ROWS, 128), F32),
            VMEM((8, 2, A_ROWS, 128), F32),
            VMEM((2, 4, 2, 2, B_ROWS, 128), F32),
            VMEM((4, 2, 2, B_ROWS, 128), F32),
            VMEM((16, A_ROWS, 128), F32),
            VMEM((4, A_ROWS, 128), F32),
            VMEM((4, 4, 2, B_ROWS, 128), F32),
            VMEM((8, B_ROWS, 128), F32),
            VMEM((8 * SPREAD, 128), F32),
            VMEM((4, SPREAD, 128), F32),
            VMEM((8, 128), F32),
            VMEM((8, 128), F32),
            VMEM((16, 128), F32),
            VMEM((272, 128), F32),
            VMEM((16, 128), F32),
            VMEM((8, 16, 128), F32),
            dma, dma((3,)), dma((4,)),
            dma, dma((8,)), dma, dma((4,)), dma, dma, dma, dma((2, 2, 4)),
            dma((2,)), dma, dma((2,)), dma, dma, dma, dma, dma, dma, dma, dma, dma, dma, dma,
        ],
        compiler_params=pltpu.CompilerParams(
            collective_id=0, has_side_effects=True, vmem_limit_bytes=64 * 1024 * 1024 - 65536
        ),
        name="reduce",
    )(inputs.T, cotangent, matrix, row_factor, row_rest)
    new_matrix, new_momentum, new_row, new_col = pl.pallas_call(
        finish_kernel,
        out_shape=(
            jax.ShapeDtypeStruct(matrix.shape, F32),
            jax.ShapeDtypeStruct(matrix.shape, F32),
            jax.ShapeDtypeStruct((3,), F32),
            jax.ShapeDtypeStruct((36, 128), F32),
        ),
        in_specs=[vmem, vmem, vmem, smem, smem, vmem, vmem],
        out_specs=(vmem, vmem, smem, vmem),
        name="finish",
    )(sums, matrix, momentum, row_factor, row_rest, col_factor.reshape(36, 128), col_rest.reshape(36, 128))
    return (new_matrix, new_momentum, new_row, new_col.reshape(4608))


def solution(mesh):
    placed = (
        P("dp", None),
        P("dp", "mp"),
        P("dp", "mp"),
        P("dp", "mp"),
        P("dp"),
        P("mp"),
        P("dp"),
        P("mp"),
    )
    return jax.shard_map(
        on_device,
        mesh=mesh,
        in_specs=placed,
        out_specs=(P("dp", "mp"), P("dp", "mp"), P("dp"), P("mp")),
        check_vma=False,
    )
```

time: 65.6 us -> 53.7 us (0.82)
  local copies, waits for them, and re-layouts: 6 us -> 0 us
  Pallas kernels: 58.7 us -> 52.9 us
    unnamed x12 -> x0, local copies, waits for them, and re-layouts: 6 us -> none
    pallas_call x1, Pallas kernels: 56.9 us -> 51.1 us  [on_device(): pl.pallas_call(reduce_kernel, out_shape=jax.ShapeDtypeStruct((SUMS + 8, 1...]
where the time goes in v2:
time: 53.7 us; the launch traced here: 53.5 us
  Pallas kernels  52.9 us (99%)
  between operations  0.64 us (1%)
    pallas_call x1, Pallas kernels, on_device(): pl.pallas_call(reduce_kernel, out_shape=jax.ShapeDtypeStruct((SUMS + 8, 1...  51.1 us
    pallas_call x1, Pallas kernels, on_device(): pl.pallas_call(finish_kernel, out_shape=(jax.ShapeDtypeStruct(matrix.shap...  1.75 us

profile of v2, /device:TPU:1, one launch (start us, length us, event | category | flops | bytes accessed | tf_op | source)
XLA Modules:
  0.0 53.5 jit_solution(4868583156801519352)
XLA Ops:
  0.6 51.1 %reduce.1.sums_ref = f32[200,128]{1,0:T(8,128)} custom-call(bf16[192,480]{1,0:T(8,128)(2,1)} %bitcast.4, bf16[480,4608]{1,0:T(8,128)(2,1)} %cot_hbm.1, f32[3,4608]{1,0:T(4,128)} %matrix_ref.1, f32[3]{0:T(128)} %row_factor_ref.1, f32[3]{0:T(128)} %row_rest_ref.1), custom_call_target="tpu_custom_call" | custom-call | tf_op jit(solution)/shard_map/reduce/pallas_call | solution.py:450
  51.8 1.8 %finish.1 = (f32[3,4608]{1,0:T(4,128)}, f32[3,4608]{1,0:T(4,128)}, f32[3]{0:T(128)}, f32[36,128]{1,0:T(8,128)}) custom-call(f32[200,128]{1,0:T(8,128)} %reduce.1.sums_ref, f32[3,4608]{1,0:T(4,128)} %matrix_ref.1, f32[3,4608]{1,0:T(4,128)} %momentum_ref.1, f32[3]{0:T(128)} %row_factor_ref.1, f32[3]{0:T(128)} %row_rest_ref.1, f32[36,128]{1,0:T(8,128)} %bitcast.5, ...), custom_call_target="tpu_custom_call" | custom-call | tf_op jit(solution)/shard_map/finish/pallas_call | solution.py:487

commit v3 on v2

--- a/solution.py
+++ b/solution.py
@@ -55,8 +55,9 @@
 
 
 def reduce_kernel(
-    inputs_hbm, cot_hbm, matrix_hbm, row_factor_hbm, row_rest_hbm, out_ref,
-    inp, matrix_ref, row_factor_ref, row_rest_ref, lhs, cot, part, sib, qpart, qsib, ring, zrecv, zq, yq,
+    inputs_hbm, cot_hbm, matrix_hbm, row_factor_hbm, row_rest_hbm, momentum_hbm, col_factor_hbm, col_rest_hbm,
+    new_matrix_ref, new_momentum_ref, new_row_ref, new_col_ref,
+    inp, matrix_ref, row_factor_ref, row_rest_ref, momentum_ref, col_factor_ref, col_rest_ref, sums_ref, lhs, cot, part, sib, qpart, qsib, ring, zrecv, zq, yq,
     spread, gathered, small, small_recv, m1, p1, m2, p2,
     in_sem, late_sem, cot_sem, sib_ss, sib_rs, qsib_ss, qsib_rs, small_ss, small_rs, ring_ss, ring_rs,
     z_ss, z_rs, zq_ss, zq_rs, yq_ss, yq_rs, g_ss, g_rs, g_own, p1_ss, p1_rs, p2_ss, p2_rs, p2_own,
@@ -81,7 +82,14 @@
     in_copy.start()
     late_copies = []
     for n, (src, dst) in enumerate(
-        ((matrix_hbm, matrix_ref), (row_factor_hbm, row_factor_ref), (row_rest_hbm, row_rest_ref))
+        (
+            (matrix_hbm, matrix_ref),
+            (row_factor_hbm, row_factor_ref),
+            (row_rest_hbm, row_rest_ref),
+            (momentum_hbm, momentum_ref),
+            (col_factor_hbm, col_factor_ref),
+            (col_rest_hbm, col_rest_ref),
+        )
     ):
         late_copies.append(pltpu.make_async_copy(src, dst, late_sem.at[n]))
     cot_copies = []
@@ -393,8 +401,8 @@
 
     landed(p2.at[pl.ds(0, 7)], p2_rs)
     for qq in range(4):
-        out_ref[qq * SPREAD : (qq + 1) * SPREAD, :] = gathered[qq]
-        out_ref[GATHERED + qq * 16 : GATHERED + qq * 16 + 16, :] = p2[qq] + p2[4 + qq]
+        sums_ref[qq * SPREAD : (qq + 1) * SPREAD, :] = gathered[qq]
+        sums_ref[GATHERED + qq * 16 : GATHERED + qq * 16 + 16, :] = p2[qq] + p2[4 + qq]
     all_y = p2[0, 8:16, :]
     for yy in range(1, 8):
         all_y = all_y + p2[yy, 8:16, :]
@@ -402,13 +410,8 @@
     for qq in range(1, 4):
         same_h = same_h + p2[4 * h + qq, 8:16, :]
     mine = jnp.sum(jnp.where(lane8 == 2 * q + c, same_h, 0.0), axis=1, keepdims=True)
-    out_ref[SUMS : SUMS + 8, :] = jnp.where(sub8 < 4, all_y, jnp.broadcast_to(mine, (8, 128)))
-
-
-def finish_kernel(
-    sums_ref, matrix_ref, momentum_ref, row_factor_ref, row_rest_ref, col_factor_ref, col_rest_ref,
-    new_matrix_ref, new_momentum_ref, new_row_ref, new_col_ref,
-):
+    sums_ref[SUMS : SUMS + 8, :] = jnp.where(sub8 < 4, all_y, jnp.broadcast_to(mine, (8, 128)))
+
     entries = float(ROWS) * float(BLOCK_COLS)
     total = sums_ref[SUMS + 1 : SUMS + 2, :]
     matrix_sq = sums_ref[SUMS + 2 : SUMS + 3, :]
@@ -422,8 +425,7 @@
         return jnp.where(sub == 0, ref[0], jnp.where(sub == 1, ref[1], ref[2]))
 
     new_row = beta_two * down(row_factor_ref) + (1.0 - beta_two) * ((row_sums + down(row_rest_ref)) / FULL_COLS)
-    for j in range(3):
-        new_row_ref[j] = new_row[j, 0]
+    new_row_ref[0:3, :] = new_row
     row_scale = lax.rsqrt(new_row / row_mean) * step
     for qq in range(4):
         at = slice(qq * LANE_TILES, (qq + 1) * LANE_TILES)
@@ -442,21 +444,47 @@
             new_matrix_ref[:, b : b + 128] = matrix_ref[:, b : b + 128] - new_momentum
 
 
+def place_kernel(
+    matrix_ref, momentum_ref, row_ref, col_ref, new_matrix_ref, new_momentum_ref, new_row_ref, new_col_ref, sem
+):
+    copies = []
+    for n, (src, dst) in enumerate(
+        ((matrix_ref, new_matrix_ref), (momentum_ref, new_momentum_ref), (col_ref, new_col_ref))
+    ):
+        copy = pltpu.make_async_copy(src, dst, sem.at[n])
+        copy.start()
+        copies.append(copy)
+    for j in range(3):
+        new_row_ref[j] = row_ref[j : j + 1, 0:1][0, 0]
+    for copy in copies:
+        copy.wait()
+
+
 def on_device(inputs, cotangent, matrix, momentum, row_factor, col_factor, row_rest, col_rest):
     vmem = pl.BlockSpec(memory_space=VMEM)
     smem = pl.BlockSpec(memory_space=pltpu.SMEM)
     hbm = pl.BlockSpec(memory_space=pltpu.HBM)
     dma = pltpu.SemaphoreType.DMA
-    sums = pl.pallas_call(
+    held = pltpu.with_memory_space_constraint
+    done = pl.pallas_call(
         reduce_kernel,
-        out_shape=jax.ShapeDtypeStruct((SUMS + 8, 128), F32),
-        in_specs=[hbm] * 5,
-        out_specs=vmem,
+        out_shape=(
+            jax.ShapeDtypeStruct(matrix.shape, F32),
+            jax.ShapeDtypeStruct(matrix.shape, F32),
+            jax.ShapeDtypeStruct((8, 128), F32),
+            jax.ShapeDtypeStruct((36, 128), F32),
+        ),
+        in_specs=[hbm] * 8,
+        out_specs=(vmem,) * 4,
         scratch_shapes=[
             VMEM((ROWS, 480), jnp.bfloat16),
             VMEM((3, 4608), F32),
             pltpu.SMEM((3,), F32),
             pltpu.SMEM((3,), F32),
+            VMEM((3, 4608), F32),
+            VMEM((36, 128), F32),
+            VMEM((36, 128), F32),
+            VMEM((SUMS + 8, 128), F32),
             VMEM((ROWS, 480), jnp.bfloat16),
             VMEM((4, 480, GROUP), jnp.bfloat16),
             VMEM((2, 8, 2, A_ROWS, 128), F32),
@@ -475,27 +503,36 @@
             VMEM((272, 128), F32),
             VMEM((16, 128), F32),
             VMEM((8, 16, 128), F32),
-            dma, dma((3,)), dma((4,)),
+            dma, dma((6,)), dma((4,)),
             dma, dma((8,)), dma, dma((4,)), dma, dma, dma, dma((2, 2, 4)),
             dma((2,)), dma, dma((2,)), dma, dma, dma, dma, dma, dma, dma, dma, dma, dma, dma,
         ],
         compiler_params=pltpu.CompilerParams(
-            collective_id=0, has_side_effects=True, vmem_limit_bytes=64 * 1024 * 1024 - 65536
+            collective_id=0, has_side_effects=True, vmem_limit_bytes=40 * 1024 * 1024
         ),
         name="reduce",
-    )(inputs.T, cotangent, matrix, row_factor, row_rest)
+    )(
+        *[
+            held(v, pltpu.HBM)
+            for v in (
+                inputs.T, cotangent, matrix, row_factor, row_rest, momentum,
+                col_factor.reshape(36, 128), col_rest.reshape(36, 128),
+            )
+        ]
+    )
     new_matrix, new_momentum, new_row, new_col = pl.pallas_call(
-        finish_kernel,
+        place_kernel,
         out_shape=(
             jax.ShapeDtypeStruct(matrix.shape, F32),
             jax.ShapeDtypeStruct(matrix.shape, F32),
             jax.ShapeDtypeStruct((3,), F32),
             jax.ShapeDtypeStruct((36, 128), F32),
         ),
-        in_specs=[vmem, vmem, vmem, smem, smem, vmem, vmem],
-        out_specs=(vmem, vmem, smem, vmem),
-        name="finish",
-    )(sums, matrix, momentum, row_factor, row_rest, col_factor.reshape(36, 128), col_rest.reshape(36, 128))
+        in_specs=[vmem] * 4,
+        out_specs=(hbm, hbm, smem, hbm),
+        scratch_shapes=[dma((3,))],
+        name="place",
+    )(*[held(v, VMEM) for v in done])
     return (new_matrix, new_momentum, new_row, new_col.reshape(4608))
 
 

time: 53.7 us -> 52.6 us (0.980)
  Pallas kernels: 52.9 us -> 51.8 us
    pallas_call x2, Pallas kernels: 52.9 us -> 51.8 us  [the longest x1 50.6 us: on_device(): pl.pallas_call(reduce_kernel, out_shape=(jax.ShapeDtypeStruct(matrix.shap...]
where the time goes in v3:
time: 52.6 us; the launch traced here: 52.4 us
  Pallas kernels  51.8 us (98%)
  between operations  0.64 us (1%)
    pallas_call x1, Pallas kernels, on_device(): pl.pallas_call(reduce_kernel, out_shape=(jax.ShapeDtypeStruct(matrix.shap...  50.6 us
    pallas_call x1, Pallas kernels, on_device(): pl.pallas_call(place_kernel, out_shape=(jax.ShapeDtypeStruct(matrix.shape...  1.2 us

profile of v3, /device:TPU:1, one launch (start us, length us, event | category | flops | bytes accessed | tf_op | source)
XLA Modules:
  0.0 52.4 jit_solution(7404272339914699539)
XLA Ops:
  0.6 50.6 %reduce.1 = (f32[3,4608]{1,0:T(4,128)S(1)}, f32[3,4608]{1,0:T(4,128)S(1)}, f32[8,128]{1,0:T(8,128)S(1)}, f32[36,128]{1,0:T(8,128)S(1)}) custom-call(bf16[192,480]{1,0:T(8,128)(2,1)} %bitcast.4, bf16[480,4608]{1,0:T(8,128)(2,1)} %cot_hbm.1, f32[3,4608]{1,0:T(4,128)} %matrix_hbm.1, f32[3]{0:T(128)} %row_factor_hbm.1, f32[3]{0:T(128)} %row_rest_hbm.1, ...), custom_call_target="tpu_custom_call" | custom-call | tf_op jit(solution)/shard_map/reduce/pallas_call | solution.py:469
  51.2 1.2 %place.1 = (f32[3,4608]{1,0:T(4,128)}, f32[3,4608]{1,0:T(4,128)}, f32[3]{0:T(128)}, f32[36,128]{1,0:T(8,128)}) custom-call(f32[3,4608]{1,0:T(4,128)S(1)} %get-tuple-element.12.matrix_ref, f32[3,4608]{1,0:T(4,128)S(1)} %get-tuple-element.13.momentum_ref, f32[8,128]{1,0:T(8,128)S(1)} %get-tuple-element.14.row_ref, f32[36,128]{1,0:T(8,128)S(1)} %get-tuple-element.15.col_ref), custom_call_target="tpu_custom_call" | custom-call | tf_op jit(solution)/shard_map/place/pallas_call | solution.py:523

commit v4 on v3

--- a/solution.py
+++ b/solution.py
@@ -495,7 +495,7 @@
             VMEM((4, A_ROWS, 128), F32),
             VMEM((4, 4, 2, B_ROWS, 128), F32),
             VMEM((8, B_ROWS, 128), F32),
-            VMEM((8 * SPREAD, 128), F32),
+            VMEM((9 * SPREAD, 128), F32),
             VMEM((4, SPREAD, 128), F32),
             VMEM((8, 128), F32),
             VMEM((8, 128), F32),

time: 52.6 us -> 52.6 us (level)
  no operation moved by 1% of the time
where the time goes in v4:
time: 52.6 us; the launch traced here: 52.4 us
  Pallas kernels  51.8 us (98%)
  between operations  0.64 us (1%)
    pallas_call x1, Pallas kernels, on_device(): pl.pallas_call(reduce_kernel, out_shape=(jax.ShapeDtypeStruct(matrix.shap...  50.6 us
    pallas_call x1, Pallas kernels, on_device(): pl.pallas_call(place_kernel, out_shape=(jax.ShapeDtypeStruct(matrix.shape...  1.2 us

profile of v4, /device:TPU:1, one launch (start us, length us, event | category | flops | bytes accessed | tf_op | source)
XLA Modules:
  0.0 52.4 jit_solution(8572748592085488402)
XLA Ops:
  0.6 50.6 %reduce.1 = (f32[3,4608]{1,0:T(4,128)S(1)}, f32[3,4608]{1,0:T(4,128)S(1)}, f32[8,128]{1,0:T(8,128)S(1)}, f32[36,128]{1,0:T(8,128)S(1)}) custom-call(bf16[192,480]{1,0:T(8,128)(2,1)} %bitcast.4, bf16[480,4608]{1,0:T(8,128)(2,1)} %cot_hbm.1, f32[3,4608]{1,0:T(4,128)} %matrix_hbm.1, f32[3]{0:T(128)} %row_factor_hbm.1, f32[3]{0:T(128)} %row_rest_hbm.1, ...), custom_call_target="tpu_custom_call" | custom-call | tf_op jit(solution)/shard_map/reduce/pallas_call | solution.py:469
  51.2 1.2 %place.1 = (f32[3,4608]{1,0:T(4,128)}, f32[3,4608]{1,0:T(4,128)}, f32[3]{0:T(128)}, f32[36,128]{1,0:T(8,128)}) custom-call(f32[3,4608]{1,0:T(4,128)S(1)} %get-tuple-element.12.matrix_ref, f32[3,4608]{1,0:T(4,128)S(1)} %get-tuple-element.13.momentum_ref, f32[8,128]{1,0:T(8,128)S(1)} %get-tuple-element.14.row_ref, f32[36,128]{1,0:T(8,128)S(1)} %get-tuple-element.15.col_ref), custom_call_target="tpu_custom_call" | custom-call | tf_op jit(solution)/shard_map/place/pallas_call | solution.py:523
